TPU v7x, 128 devices: a whole 4x4x4 slice. The times are simulated.
128 devices in a mesh: lat: 8 (over z, core), lon: 16 (over x, y).
Axes of the slice: x: 4, y: 4, z: 4, core: 2. Of those that a mesh axis runs over, the one named last changes fastest.
Arguments:
- obs_values: bfloat16 [128, 128, 64, 32], P(('lat', 'lon')), may hold values from -6 to 6
- kernel_weights: bfloat16 [128, 128, 64, 128], P(('lat', 'lon')), may hold values from 0.0099487305 to 1
- pixel_blocks: int32 [128, 128, 64], P(('lat', 'lon')), may hold values from 0 to 127
- obs_counts: int32 [128, 128], P(('lat', 'lon')), may hold values from 1 to 64, as said below
- kernel_one: float32 [3, 3, 64, 33], replicated, may hold values from -0.375 to 0.375
- kernel_two: float32 [3, 3, 64, 64], replicated, may hold values from -0.25 to 0.25
- cotangent: bfloat16 [64, 64, 2048], P(None, 'lat', 'lon'), may hold values from -0.015625 to 0.015625
Outputs:
- features: bfloat16 [64, 64, 2048], P(None, 'lat', 'lon')
- grad_kernel_one: float32 [3, 3, 64, 33], replicated
- grad_kernel_two: float32 [3, 3, 64, 64], replicated
Inputs may be any that keep to these rules, and one draw needn't show every extreme that they name: `obs_counts`: every count is at least 1 and at most 64; in every draw some tile receives exactly 64 observations from every instrument shard, and the loads of tiles differ.
All inputs are finite; a program needn't handle non-finite values.
Results may differ from a plain program's by a relative error of at most 0.0014.
Values may be sent and summed in bfloat16 or wider, within the bound.
A program may use at most 64 MiB of HBM per device.

v0:
```python
import jax
import jax.numpy as jnp
from jax import lax
from jax.experimental import pallas as pl
from jax.experimental.pallas import tpu as pltpu
from jax.sharding import PartitionSpec as P

MESH = pl.DeviceIdType.MESH
F32, BF16 = jnp.float32, jnp.bfloat16
N = 128
CAP = 64
GROUP = 16
STEPS = N // GROUP
SLOTS = GROUP * CAP
ROWS = 32
C_OBS = 32


def position():
    return lax.axis_index("lat"), lax.axis_index("lon")


def partner(lat, lon, ordinal, sign):
    mixed = lax.rem(ordinal * 37, N)
    core = lax.rem(mixed, 2)
    dz = lax.rem(mixed // 2, 4)
    dx = lax.rem(mixed // 8, 4)
    dy = mixed // 32
    z = lax.rem(lat // 2 + sign * dz + 4, 4)
    c = lax.rem(lat + core, 2)
    x = lax.rem(lon // 4 + sign * dx + 4, 4)
    y = lax.rem(lon + sign * dy + 4, 4)
    return z * 2 + c, x * 4 + y


def greet_all(lat, lon):
    barrier = pltpu.get_barrier_semaphore()

    def greet(step, carry):
        to_lat = lax.rem(lat + step, 8)
        for d in range(16):
            @pl.when(jnp.logical_or(step > 0, d > 0))
            def _():
                pl.semaphore_signal(
                    barrier, inc=1, device_id=(to_lat, lax.rem(lon + d, 16)), device_id_type=MESH
                )
        return carry

    lax.fori_loop(0, 8, greet, 0)
    return barrier


def pack_values(values_ref, wide_ref, turned_ref, packed_ref):
    wide_ref[...] = values_ref[...].astype(F32)
    for i in range(16):
        pair = jnp.concatenate([wide_ref[:, i, :], wide_ref[:, 16 + i, :]], axis=0)
        turned_ref[:, i, :] = pair.T
    packed_ref[...] = turned_ref[...].astype(BF16)


def pack_codes(blocks_ref, counts_ref, codes_ref):
    slot = lax.broadcasted_iota(jnp.int32, (CAP, N), 0)
    code = jnp.where(slot < counts_ref[...], blocks_ref[...], 4 * ROWS)
    turned = jnp.concatenate([code, code], axis=0).astype(F32).T.astype(jnp.int32)
    codes_ref[:, 0, :] = turned


def spread_group(step, got_w, got_v, got_c, perm_ref, lhs_ref, rhs_ref, acc_ref):
    first = step * GROUP
    lane = lax.broadcasted_iota(jnp.int32, (1, N), 1)
    codes = got_c[pl.ds(first, GROUP), 0, :]
    row_parts, value_parts = [], []
    for p in range(GROUP // 2):
        even, odd = codes[2 * p : 2 * p + 1], codes[2 * p + 1 : 2 * p + 2]
        row_parts.append(jnp.where(lane < CAP, even, odd))
        one = got_v[first + 2 * p].astype(F32)
        two = got_v[first + 2 * p + 1].astype(F32)
        upper = jnp.where(lane < CAP, one, pltpu.roll(two, CAP, 1))
        lower = jnp.where(lane < CAP, pltpu.roll(one, CAP, 1), two)
        value_parts.append(jnp.concatenate([upper, lower], axis=0))
    row_of = jnp.broadcast_to(jnp.concatenate(row_parts, axis=1) // 4, (C_OBS, SLOTS)).astype(F32).astype(BF16)
    values = jnp.concatenate(value_parts, axis=1).astype(BF16)
    zero = jnp.zeros_like(values)
    for r in range(ROWS):
        lhs_ref[r * C_OBS : (r + 1) * C_OBS, :] = jnp.where(row_of == jnp.array(r, BF16), values, zero)
    rows = lax.broadcasted_iota(jnp.int32, (ROWS, SLOTS), 0).astype(F32).astype(BF16)
    lhs_ref[ROWS * C_OBS :, :] = jnp.where(row_of == rows, jnp.ones_like(values), zero)
    quarter = lax.rem(codes, 4).astype(F32).T
    lane_quarter = (lax.broadcasted_iota(jnp.int32, (CAP, N), 1) // 32).astype(F32)
    for s in range(GROUP):
        keep = jnp.where(quarter[:CAP, s : s + 1] == lane_quarter, 1.0, 0.0).astype(BF16)
        pixels = jnp.dot(got_w[first + s], perm_ref[...], preferred_element_type=F32).astype(BF16)
        for phase in range(4):
            rhs_ref[s * CAP : (s + 1) * CAP, phase * N : (phase + 1) * N] = (
                pixels[:, phase * N : (phase + 1) * N] * keep
            )
    acc_ref[...] += jnp.dot(lhs_ref[...], rhs_ref[...], preferred_element_type=F32)


def send_to(source, target, sent, came, device):
    return pltpu.make_async_remote_copy(
        src_ref=source, dst_ref=target, send_sem=sent, recv_sem=came, device_id=device, device_id_type=MESH
    )


def all_sum(lat, lon, part_ref, total_ref, by_lat, by_y, by_x, sent, came):
    x, y = lon // 4, lax.rem(lon, 4)
    rows = lambda at: pl.ds(pl.multiple_of(8 * at, 8), 8)
    copies = []
    for d in range(1, 8):
        to = lax.rem(lat + d, 8)
        copies.append(send_to(part_ref.at[rows(to)], by_lat.at[d], sent.at[d], came.at[d], (to, lon)))
    for copy in copies:
        copy.start()
    for copy in copies:
        copy.wait()
    total = part_ref[rows(lat), :]
    for d in range(1, 8):
        total = total + by_lat[d]
    for base, slots, here in ((8, by_y, y), (12, by_x, x)):
        slots[here] = total
        copies = []
        for d in range(1, 4):
            to_lon = x * 4 + lax.rem(y + d, 4) if base == 8 else lax.rem(x + d, 4) * 4 + y
            copies.append(send_to(slots.at[here], slots.at[here], sent.at[base + d], came.at[base + d], (lat, to_lon)))
        for copy in copies:
            copy.start()
        for copy in copies:
            copy.wait()
        total = (slots[0] + slots[1]) + (slots[2] + slots[3])
    total_ref[rows(lat), :] = total
    copies = []
    for d in range(1, 8):
        to = lax.rem(lat + d, 8)
        copies.append(send_to(total_ref.at[rows(lat)], total_ref.at[rows(lat)], sent.at[16 + d], came.at[16 + d], (to, lon)))
    for copy in copies:
        copy.start()
    for copy in copies:
        copy.wait()

CH = 64
STEP_ONE = 5 * C_OBS
STEP_TWO = 3 * CH


def halves(value):
    high = value.astype(BF16)
    return high, (value - high.astype(F32)).astype(BF16)


def dot_nt(a, b):
    return lax.dot_general(a, b, (((1,), (1,)), ((), ())), preferred_element_type=F32)


def dot(a, b):
    return jnp.dot(a, b, preferred_element_type=F32)


def lanes(rows):
    return lax.broadcasted_iota(jnp.int32, (rows, N), 1)


def pack_column(total, place, column):
    return jnp.where(lanes(total.shape[0]) == place, jnp.broadcast_to(column, total.shape), total)


def enter_west(value, column):
    moved = pltpu.roll(value, 1, 1)
    return jnp.where(lanes(value.shape[0]) == 0, jnp.broadcast_to(column, value.shape), moved)


def enter_east(value, column):
    moved = pltpu.roll(value, N - 1, 1)
    return jnp.where(lanes(value.shape[0]) == N - 1, jnp.broadcast_to(column, value.shape), moved)


def arrange_kernels(one_ref, two_ref, wide_one, wide_adj, wide_two, left_one, left_adj, left_two):
    wide_one[...] = jnp.zeros_like(wide_one)
    wide_adj[...] = jnp.zeros_like(wide_adj)
    for a in range(3):
        for tap in range(5):
            row = a * STEP_ONE + tap * C_OBS
            thin = 3 * STEP_ONE + a * 8 + tap
            for half, e in ((0, tap), (1, tap - 2)):
                if 0 <= e < 3:
                    at = slice(half * CH, half * CH + CH)
                    wide_one[row : row + C_OBS, at] = one_ref[a, e, :C_OBS, :]
                    wide_one[thin : thin + 1, at] = one_ref[a, e, C_OBS:, :]
        for e in range(3):
            at = (a * 3 + e) * CH
            wide_two[:, at : at + CH] = two_ref[a, e]
    for lower in range(2):
        for east in range(2):
            for down in range(lower + 1):
                for right in range(east + 1):
                    a = 1 if lower == 0 else 2 - 2 * down
                    e = 1 if east == 0 else 2 - 2 * right
                    row, col = (down * 2 + right) * CH, (lower * 2 + east) * CH
                    wide_adj[row : row + CH, col : col + CH] = two_ref[a, e]
    for wide, left, turn in ((wide_one, left_one, True), (wide_adj, left_adj, True), (wide_two, left_two, False)):
        value = wide[...].T if turn else wide[...]
        high, low = halves(value)
        rows = value.shape[0]
        left[:rows, :] = high
        left[rows:, :] = low


def arrange_cotangent(cot_ref, wide_cot, cot, cot_col):
    wide_cot[...] = cot_ref[...].astype(F32)
    packed = jnp.zeros((CH, N), F32)
    for g in range(8):
        value = wide_cot[:, g, :]
        cot[g] = value
        packed = pack_column(packed, g, value[:, :1])
    cot_col[...] = packed


def back_to_activation(lat, cot, from_south, from_east, from_corner, right, left_adj, grad_act):
    cot[8] = jnp.where(lat < 7, from_south[...], 0.0)
    edge = from_east[...]
    for g in range(9):
        column = edge[:, g : g + 1] if g < 8 else jnp.where(lat < 7, from_corner[:, :1], 0.0)
        right[g] = enter_east(cot[g], column)

    def pair(p, carry):
        stack = [
            jnp.concatenate([cot[g], right[g], cot[g + 1], right[g + 1]], axis=0).astype(BF16)
            for g in (2 * p, 2 * p + 1)
        ]
        both = dot(left_adj[...], jnp.concatenate(stack, axis=1))
        both = both[:256] + both[256:]
        grad_act[2 * p] = both[:, :N]
        grad_act[2 * p + 1] = both[:, N:]
        return carry

    lax.fori_loop(0, 4, pair, 0)


def split_row(r, rows_of, edge, high_ref, low_ref):
    phases = [rows_of(phase) for phase in range(4)]
    taps = [enter_west(phases[3], edge)] + phases
    high, low = halves(jnp.concatenate(taps, axis=0))
    high_ref[r] = high
    low_ref[r] = low


def field_edges(acc_ref, edge_ref):
    packed = jnp.zeros((C_OBS, N), F32)
    for r in range(ROWS):
        packed = pack_column(packed, r, acc_ref[r * C_OBS : (r + 1) * C_OBS, 4 * N - 1 :])
    edge_ref[:C_OBS, :] = packed
    edge_ref[C_OBS:, :] = acc_ref[ROWS * C_OBS :, 3 * N :]


def split_field(lat, acc_ref, north, north_thin, from_west, from_corner, thin, high_ref, low_ref, thin_high, thin_low):
    for r in range(ROWS):
        split_row(
            r + 1,
            lambda phase, r=r: acc_ref[r * C_OBS : (r + 1) * C_OBS, phase * N : (phase + 1) * N],
            from_west[:C_OBS, r : r + 1], high_ref, low_ref,
        )
    inside = lat > 0
    split_row(
        0,
        lambda phase: jnp.where(inside, north[:, phase * N : (phase + 1) * N], 0.0),
        jnp.where(inside, from_corner[:C_OBS, ROWS - 1 : ROWS], 0.0), high_ref, low_ref,
    )
    thin[...] = jnp.zeros_like(thin)
    for phase in range(4):
        at = slice(phase * N, (phase + 1) * N)
        thin[1 : ROWS + 1, phase + 1, :] = acc_ref[ROWS * C_OBS :, at]
        thin[0, phase + 1 : phase + 2, :] = jnp.where(inside, north_thin[7:8, at], 0.0)
    thin[1 : ROWS + 1, 0, :] = enter_west(acc_ref[ROWS * C_OBS :, 3 * N :], from_west[C_OBS:, N - 1 :])
    corner = enter_west(north_thin[7:8, 3 * N :], from_corner[2 * C_OBS - 1 :, N - 1 :])
    thin[0, 0:1, :] = jnp.where(inside, corner, 0.0)
    for h in range(ROWS // 2):
        rows = [thin[2 * h], thin[2 * h + 1], thin[2 * h + 2], jnp.zeros((8, N), F32)]
        high, low = halves(jnp.concatenate(rows, axis=0))
        thin_high[h] = high
        thin_low[h] = low


def taps_one(h, field, thin):
    return jnp.concatenate([field[2 * h], field[2 * h + 1], field[2 * h + 2], thin[h]], axis=0)


def taps_two(h, act):
    return jnp.concatenate([act[2 * h], act[2 * h + 1], act[2 * h + 2]], axis=0)


def beside(function, p, *refs):
    return jnp.concatenate([function(2 * p, *refs), function(2 * p + 1, *refs)], axis=1)


def first_layer(field_high, field_low, thin_high, thin_low, left_one, pre, act):
    def pair(p, carry):
        both = dot(left_one[...], beside(taps_one, p, field_high, thin_high))
        out = both[:N] + both[N:] + dot(left_one[:N, :], beside(taps_one, p, field_low, thin_low))
        active = out / (1.0 + jnp.exp(-out))
        for k in range(2):
            pre[2 * p + k] = out[:, k * N : (k + 1) * N]
            act[2 * p + k] = active[:, k * N : (k + 1) * N]
        return carry

    lax.fori_loop(0, ROWS // 4, pair, 0)


def first_gradient(field_high, field_low, thin_high, thin_low, pre, grad_act):
    def row(h, g, lower):
        value = pre[h]
        s = 1.0 / (1.0 + jnp.exp(-value))
        return grad_act[g, lower * N : (lower + 1) * N, :] * (s * (1.0 + value * (1.0 - s)))

    def pair(p, total):
        grad = jnp.concatenate([row(2 * p, p, 0), row(2 * p + 1, p, 1)], axis=1)
        high, low = halves(grad)
        field = beside(taps_one, p, field_high, thin_high)
        both = dot_nt(jnp.concatenate([high, low], axis=0), field)
        return total + (both[:N] + both[N:]) + dot_nt(high, beside(taps_one, p, field_low, thin_low))

    return lax.fori_loop(0, ROWS // 4, pair, jnp.zeros((N, 4 * N), F32))


def activation_edges(act, edge_ref):
    packed = jnp.zeros((CH, N), F32)
    for y in range(ROWS // 2):
        packed = pack_column(packed, y, act[y, CH:, N - 1 :])
    edge_ref[...] = packed


def split_activation(lat, act, north, from_west, from_corner, high_ref, low_ref):
    def one(place, value, column):
        high, low = halves(jnp.concatenate([enter_west(value[CH:], column), value], axis=0))
        high_ref[place] = high
        low_ref[place] = low

    for y in range(ROWS // 2):
        one(y + 1, act[y], from_west[:, y : y + 1])
    last = ROWS // 2 - 1
    one(0, jnp.where(lat > 0, north[...], 0.0), jnp.where(lat > 0, from_corner[:, last : last + 1], 0.0))


def second_layer(act_high, act_low, left_two, cot, wide_features):
    total = jnp.zeros((CH, 9 * CH), F32)
    for p in range(4):
        high, low = beside(taps_two, p, act_high), beside(taps_two, p, act_low)
        both = dot(left_two[...], high)
        out = both[:CH] + both[CH:] + dot(left_two[:CH, :], low)
        for k in range(2):
            wide_features[:, 2 * p + k, :] = out[:, k * N : (k + 1) * N]
        grad = jnp.concatenate([cot[2 * p], cot[2 * p + 1]], axis=1).astype(BF16)
        total = total + (dot_nt(grad, high) + dot_nt(grad, low))
    return total


def pack_gradients(one, two, part_ref):
    lane = lax.broadcasted_iota(jnp.int32, (CH, 4 * N), 1)
    upper, lower = one[:CH], one[CH:]
    moved = jnp.where(lane < 3 * STEP_ONE, pltpu.roll(lower, 4 * N - 2 * C_OBS, 1), pltpu.roll(lower, 4 * N - 2, 1))
    both = upper + moved
    tight = jnp.where(
        lane < 96, both,
        jnp.where(
            lane < 192, pltpu.roll(both, 4 * N - 64, 1),
            jnp.where(lane < 288, pltpu.roll(both, 4 * N - 128, 1), pltpu.roll(both, 4 * N - 192, 1)),
        ),
    )
    shifted = pltpu.roll(tight, CH, 1)
    part_ref[:, 4 * N : 7 * N] = shifted[:, : 3 * N]
    part_ref[:, : 9 * CH] = two


def unpack_gradients(total_ref, one_ref, two_ref):
    for i in range(9):
        two_ref[i] = total_ref[:, i * CH : (i + 1) * CH]
    turned = total_ref[:, 4 * N : 7 * N].T
    for i in range(9):
        one_ref[i, :C_OBS, :] = turned[CH + i * C_OBS : CH + (i + 1) * C_OBS]
        thin = CH + 9 * C_OBS + (i // 3) * 8 + i % 3
        one_ref[i, C_OBS:, :] = turned[thin : thin + 1]


def phase_picker():
    lane = jnp.arange(4 * N, dtype=jnp.int32)
    source = 4 * (lane % 32) + lane // N
    return (jnp.arange(N, dtype=jnp.int32)[:, None] == source[None, :]).astype(BF16)


class Named:
    def __init__(self, names, refs):
        self.__dict__.update(zip(names, refs))


SCRATCH = {
    "wide": pltpu.VMEM((CAP, C_OBS, N), F32),
    "turned": pltpu.VMEM((N, 16, N), F32),
    "packed": pltpu.VMEM((N, 16, N), BF16),
    "codes": pltpu.VMEM((N, 1, N), jnp.int32),
    "got_w": pltpu.VMEM((N, CAP, N), BF16),
    "got_v": pltpu.VMEM((N, 16, N), BF16),
    "got_c": pltpu.VMEM((N, 1, N), jnp.int32),
    "lhs": pltpu.VMEM((ROWS * C_OBS + ROWS, SLOTS), BF16),
    "rhs": pltpu.VMEM((SLOTS, 4 * N), BF16),
    "acc": pltpu.VMEM((ROWS * C_OBS + ROWS, 4 * N), F32),
    "wide_one": pltpu.VMEM((4 * N, N), F32),
    "wide_adj": pltpu.VMEM((256, 256), F32),
    "wide_two": pltpu.VMEM((CH, 9 * CH), F32),
    "left_one": pltpu.VMEM((256, 4 * N), BF16),
    "left_adj": pltpu.VMEM((512, 256), BF16),
    "left_two": pltpu.VMEM((N, 9 * CH), BF16),
    "wide_cot": pltpu.VMEM((CH, 8, N), F32),
    "cot": pltpu.VMEM((9, CH, N), F32),
    "cot_right": pltpu.VMEM((9, CH, N), F32),
    "cot_col": pltpu.VMEM((CH, N), F32),
    "cot_south": pltpu.VMEM((CH, N), F32),
    "cot_east": pltpu.VMEM((CH, N), F32),
    "cot_corner": pltpu.VMEM((CH, N), F32),
    "grad_act": pltpu.VMEM((8, 256, N), F32),
    "edge": pltpu.VMEM((2 * C_OBS, N), F32),
    "edge_west": pltpu.VMEM((2 * C_OBS, N), F32),
    "edge_corner": pltpu.VMEM((2 * C_OBS, N), F32),
    "north": pltpu.VMEM((C_OBS, 4 * N), F32),
    "north_thin": pltpu.VMEM((8, 4 * N), F32),
    "thin": pltpu.VMEM((ROWS + 1, 8, N), F32),
    "field_high": pltpu.VMEM((ROWS + 1, STEP_ONE, N), BF16),
    "field_low": pltpu.VMEM((ROWS + 1, STEP_ONE, N), BF16),
    "thin_high": pltpu.VMEM((ROWS // 2, 32, N), BF16),
    "thin_low": pltpu.VMEM((ROWS // 2, 32, N), BF16),
    "pre": pltpu.VMEM((ROWS // 2, N, N), F32),
    "act": pltpu.VMEM((ROWS // 2, N, N), F32),
    "act_edge": pltpu.VMEM((CH, N), F32),
    "act_west": pltpu.VMEM((CH, N), F32),
    "act_corner": pltpu.VMEM((CH, N), F32),
    "act_north": pltpu.VMEM((N, N), F32),
    "act_high": pltpu.VMEM((ROWS // 2 + 1, STEP_TWO, N), BF16),
    "act_low": pltpu.VMEM((ROWS // 2 + 1, STEP_TWO, N), BF16),
    "wide_features": pltpu.VMEM((CH, 8, N), F32),
    "part": pltpu.VMEM((CH, 7 * N), F32),
    "total": pltpu.VMEM((CH, 7 * N), F32),
    "by_lat": pltpu.VMEM((8, 8, 7 * N), F32),
    "by_y": pltpu.VMEM((4, 8, 7 * N), F32),
    "by_x": pltpu.VMEM((4, 8, 7 * N), F32),
    "sent": pltpu.SemaphoreType.DMA((3,)),
    "came_w": pltpu.SemaphoreType.DMA((STEPS,)),
    "came_v": pltpu.SemaphoreType.DMA((STEPS,)),
    "came_c": pltpu.SemaphoreType.DMA((STEPS,)),
    "own": pltpu.SemaphoreType.DMA((3,)),
    "halo_sent": pltpu.SemaphoreType.DMA((10,)),
    "halo_came": pltpu.SemaphoreType.DMA((10,)),
    "sum_sent": pltpu.SemaphoreType.DMA((24,)),
    "sum_came": pltpu.SemaphoreType.DMA((24,)),
}


def whole_kernel(
    values_ref, w_ref, blocks_ref, counts_ref, perm_ref, one_ref, two_ref, cot_ref,
    features_ref, grad_one_ref, grad_two_ref, *scratch,
):
    m = Named(SCRATCH, scratch)
    lat, lon = position()
    me = lat * 16 + lon
    barrier = greet_all(lat, lon)
    pack_values(values_ref, m.wide, m.turned, m.packed)
    pack_codes(blocks_ref, counts_ref, m.codes)
    arrange_cotangent(cot_ref, m.wide_cot, m.cot, m.cot_col)
    arrange_kernels(one_ref, two_ref, m.wide_one, m.wide_adj, m.wide_two, m.left_one, m.left_adj, m.left_two)
    m.acc[...] = jnp.zeros_like(m.acc)
    mine = [
        pltpu.make_async_copy(w_ref.at[me], m.got_w.at[0], m.own.at[0]),
        pltpu.make_async_copy(m.packed.at[me], m.got_v.at[0], m.own.at[1]),
        pltpu.make_async_copy(m.codes.at[me], m.got_c.at[0], m.own.at[2]),
    ]
    for copy in mine:
        copy.start()

    north, south = lax.rem(lat + 7, 8), lax.rem(lat + 1, 8)
    west, east = lax.rem(lon + 15, 16), lax.rem(lon + 1, 16)

    def halo(k, source, target, device):
        return send_to(source, target, m.halo_sent.at[k], m.halo_came.at[k], device)

    cot_halo = [
        halo(0, m.cot_col, m.cot_east, (lat, west)),
        halo(1, m.cot.at[0], m.cot_south, (north, lon)),
        halo(2, m.cot_col, m.cot_corner, (north, west)),
    ]
    pl.semaphore_wait(barrier, N - 1)
    for copy in cot_halo:
        copy.start()

    streams = ((w_ref, m.got_w, m.came_w), (m.packed, m.got_v, m.came_v), (m.codes, m.got_c, m.came_c))

    def send(ordinal, carry):
        to_lat, to_lon = partner(lat, lon, ordinal, 1)
        to = to_lat * 16 + to_lon
        step = ordinal // GROUP
        for k, (source, target, came) in enumerate(streams):
            send_to(source.at[to], target.at[ordinal], m.sent.at[k], came.at[step], (to_lat, to_lon)).start()
        return carry

    lax.fori_loop(1, N, send, 0)
    for copy in cot_halo:
        copy.wait()
    back_to_activation(
        lat, m.cot, m.cot_south, m.cot_east, m.cot_corner, m.cot_right, m.left_adj, m.grad_act
    )
    for copy in mine:
        copy.wait()

    def arrive(first, count, step):
        for source, target, came in streams:
            pltpu.make_async_copy(
                target.at[pl.ds(first, count)], target.at[pl.ds(first, count)], came.at[step]
            ).wait()

    def work(step, carry):
        @pl.when(step == 0)
        def _():
            arrive(1, GROUP - 1, 0)

        @pl.when(step > 0)
        def _():
            arrive(step * GROUP, GROUP, step)

        spread_group(step, m.got_w, m.got_v, m.got_c, perm_ref, m.lhs, m.rhs, m.acc)
        return carry

    lax.fori_loop(0, STEPS, work, 0)

    last = ROWS * C_OBS
    rows_halo = [
        halo(3, m.acc.at[pl.ds(last - C_OBS, C_OBS)], m.north, (south, lon)),
        halo(4, m.acc.at[pl.ds(last + ROWS - 8, 8)], m.north_thin, (south, lon)),
    ]
    edge_halo = [
        halo(5, m.edge, m.edge_west, (lat, east)),
        halo(6, m.edge, m.edge_corner, (south, east)),
    ]
    for copy in rows_halo:
        copy.start()
    field_edges(m.acc, m.edge)
    for copy in edge_halo:
        copy.start()
    for copy in edge_halo + rows_halo:
        copy.wait()
    split_field(
        lat, m.acc, m.north, m.north_thin, m.edge_west, m.edge_corner, m.thin,
        m.field_high, m.field_low, m.thin_high, m.thin_low,
    )
    field = (m.field_high, m.field_low, m.thin_high, m.thin_low)
    first_layer(*field, m.left_one, m.pre, m.act)
    act_halo = [
        halo(7, m.act.at[ROWS // 2 - 1], m.act_north, (south, lon)),
        halo(8, m.act_edge, m.act_west, (lat, east)),
        halo(9, m.act_edge, m.act_corner, (south, east)),
    ]
    act_halo[0].start()
    activation_edges(m.act, m.act_edge)
    act_halo[1].start()
    act_halo[2].start()
    grad_one = first_gradient(*field, m.pre, m.grad_act)
    for copy in act_halo:
        copy.wait()
    split_activation(lat, m.act, m.act_north, m.act_west, m.act_corner, m.act_high, m.act_low)
    grad_two = second_layer(m.act_high, m.act_low, m.left_two, m.cot, m.wide_features)
    pack_gradients(grad_one, grad_two, m.part)
    features_ref[...] = m.wide_features[...].astype(BF16)
    all_sum(lat, lon, m.part, m.total, m.by_lat, m.by_y, m.by_x, m.sum_sent, m.sum_came)
    unpack_gradients(m.total, grad_one_ref, grad_two_ref)
    for k, (_, target, _) in enumerate(streams):
        pltpu.make_async_copy(target.at[pl.ds(0, N - 1)], target.at[pl.ds(0, N - 1)], m.sent.at[k]).wait()


def on_device(
    obs_values, kernel_weights, pixel_blocks, obs_counts, kernel_one, kernel_two, cotangent
):
    vmem = pl.BlockSpec(memory_space=pltpu.VMEM)
    features, grad_one, grad_two = pl.pallas_call(
        whole_kernel,
        out_shape=(
            jax.ShapeDtypeStruct((CH, 8, N), BF16),
            jax.ShapeDtypeStruct((9, C_OBS + 1, CH), F32),
            jax.ShapeDtypeStruct((9, CH, CH), F32),
        ),
        in_specs=[vmem, pl.BlockSpec(memory_space=pl.ANY)] + [vmem] * 6,
        out_specs=(vmem, vmem, vmem),
        scratch_shapes=list(SCRATCH.values()),
        compiler_params=pltpu.CompilerParams(collective_id=0, has_side_effects=True, vmem_limit_bytes=56 << 20),
    )(
        obs_values[0].transpose(1, 2, 0),
        kernel_weights[0],
        pixel_blocks[0].T,
        obs_counts,
        phase_picker(),
        kernel_one.transpose(0, 1, 3, 2),
        kernel_two,
        cotangent,
    )
    grad_one = grad_one.reshape(3, 3, C_OBS + 1, CH).transpose(0, 1, 3, 2)
    return features, grad_one, grad_two.reshape(3, 3, CH, CH)


def solution(mesh):
    placed = (
        P(("lat", "lon"), None, None, None),
        P(("lat", "lon"), None, None, None),
        P(("lat", "lon"), None, None),
        P(("lat", "lon"), None),
        P(),
        P(),
        P(None, "lat", "lon"),
    )
    return jax.shard_map(
        on_device,
        mesh=mesh,
        in_specs=placed,
        out_specs=(P(None, "lat", "lon"), P(), P()),
        check_vma=False,
    )
```

profile of v0, /device:TPU:1, one launch (start us, length us, event | category | flops | bytes accessed | tf_op | source)
XLA Modules:
  0.0 86.1 jit_solution(6924308126058933160)
XLA Ops:
  0.6 0.7 fusion.perm_ref
  1.3 79.9 %shard_map.94 = (bf16[64,8,128]{2,1,0:T(8,128)(2,1)}, f32[9,33,64]{2,1,0:T(8,128)}, f32[9,64,64]{2,1,0:T(8,128)}) custom-call(bf16[64,32,128]{2,1,0:T(8,128)(2,1)} %bitcast.13, bf16[128,64,128]{2,1,0:T(8,128)(2,1)} %bitcast.12, s32[64,128]{1,0:T(8,128)} %bitcast.17, s32[1,128]{1,0:T(1,128)} %counts_ref.1, bf16[128,512]{1,0:T(8,128)(2,1)} %fusion.perm_ref, ...), custom_call_target="tpu_custom_call" | custom-call | tf_op jit(solution)/shard_map/pallas_call | solution.py:578
  81.2 1.6 %copy.13 = bf16[64,8,128]{2,1,0:T(8,128)(2,1)} copy(bf16[64,8,128]{2,1,0:T(8,128)(2,1)} %get-tuple-element.12) | data formatting | bytes 262144
  82.8 1.6 %copy.14 = f32[3,3,64,33]{2,3,1,0:T(8,128)} copy(f32[3,3,64,33]{2,3,1,0:T(8,128)} %bitcast.16) | data formatting | bytes 152064
  84.4 1.7 %copy.15 = f32[3,3,64,64]{3,2,1,0:T(8,128)} copy(f32[3,3,64,64]{3,2,1,0:T(8,128)} %bitcast.14) | data formatting | bytes 294912
  (1 shorter events, 0.0 us)
where the time goes:
time: 86.3 us; the launch traced here: 86.1 us
  Pallas kernels  79.9 us (93%)
  local copies, waits for them, and re-layouts  4.87 us (6%)
    pallas_call x1, Pallas kernels, on_device(): pl.pallas_call(whole_kernel, out_shape=(jax.ShapeDtypeStruct((CH, 8, N),...  79.9 us
    unnamed x3, local copies, waits for them, and re-layouts  4.87 us

commit v1 on v0

--- a/solution.py
+++ b/solution.py
@@ -10,8 +10,9 @@
 N = 128
 CAP = 64
 GROUP = 16
-STEPS = N // GROUP
+STEPS = N // GROUP - 1
 SLOTS = GROUP * CAP
+SENT = CAP + 16
 ROWS = 32
 C_OBS = 32
 
@@ -20,42 +21,32 @@
     return lax.axis_index("lat"), lax.axis_index("lon")
 
 
-def partner(lat, lon, ordinal, sign):
+def partner(lat, lon, ordinal):
     mixed = lax.rem(ordinal * 37, N)
-    core = lax.rem(mixed, 2)
-    dz = lax.rem(mixed // 2, 4)
-    dx = lax.rem(mixed // 8, 4)
-    dy = mixed // 32
-    z = lax.rem(lat // 2 + sign * dz + 4, 4)
-    c = lax.rem(lat + core, 2)
-    x = lax.rem(lon // 4 + sign * dx + 4, 4)
-    y = lax.rem(lon + sign * dy + 4, 4)
-    return z * 2 + c, x * 4 + y
-
-
-def greet_all(lat, lon):
+    z = lax.rem(lat // 2 + lax.rem(mixed // 2, 4), 4)
+    core = lax.rem(lat + lax.rem(mixed, 2), 2)
+    x = lax.rem(lon // 4 + lax.rem(mixed // 8, 4), 4)
+    y = lax.rem(lon + mixed // 32, 4)
+    return z * 2 + core, x * 4 + y
+
+
+NEAR = 22
+
+
+def greet_near(lat, lon):
     barrier = pltpu.get_barrier_semaphore()
-
-    def greet(step, carry):
-        to_lat = lax.rem(lat + step, 8)
-        for d in range(16):
-            @pl.when(jnp.logical_or(step > 0, d > 0))
-            def _():
-                pl.semaphore_signal(
-                    barrier, inc=1, device_id=(to_lat, lax.rem(lon + d, 16)), device_id_type=MESH
-                )
-        return carry
-
-    lax.fori_loop(0, 8, greet, 0)
+    for d in range(1, 16):
+        pl.semaphore_signal(barrier, inc=1, device_id=(lat, lax.rem(lon + d, 16)), device_id_type=MESH)
+    for d in range(1, 8):
+        pl.semaphore_signal(barrier, inc=1, device_id=(lax.rem(lat + d, 8), lon), device_id_type=MESH)
     return barrier
 
 
-def pack_values(values_ref, wide_ref, turned_ref, packed_ref):
-    wide_ref[...] = values_ref[...].astype(F32)
+def pack_values(wide_ref, turned_ref, message_ref):
     for i in range(16):
         pair = jnp.concatenate([wide_ref[:, i, :], wide_ref[:, 16 + i, :]], axis=0)
         turned_ref[:, i, :] = pair.T
-    packed_ref[...] = turned_ref[...].astype(BF16)
+    message_ref[:, CAP:, :] = turned_ref[...].astype(BF16)
 
 
 def pack_codes(blocks_ref, counts_ref, codes_ref):
@@ -65,36 +56,36 @@
     codes_ref[:, 0, :] = turned
 
 
-def spread_group(step, got_w, got_v, got_c, perm_ref, lhs_ref, rhs_ref, acc_ref):
-    first = step * GROUP
+def spread_group(first, group, got, got_c, perm_ref, lhs_ref, rhs_ref, acc_ref):
+    slots = group * CAP
     lane = lax.broadcasted_iota(jnp.int32, (1, N), 1)
-    codes = got_c[pl.ds(first, GROUP), 0, :]
+    codes = got_c[pl.ds(first, group), 0, :]
     row_parts, value_parts = [], []
-    for p in range(GROUP // 2):
+    for p in range(group // 2):
         even, odd = codes[2 * p : 2 * p + 1], codes[2 * p + 1 : 2 * p + 2]
         row_parts.append(jnp.where(lane < CAP, even, odd))
-        one = got_v[first + 2 * p].astype(F32)
-        two = got_v[first + 2 * p + 1].astype(F32)
+        one = got[first + 2 * p, CAP:, :].astype(F32)
+        two = got[first + 2 * p + 1, CAP:, :].astype(F32)
         upper = jnp.where(lane < CAP, one, pltpu.roll(two, CAP, 1))
         lower = jnp.where(lane < CAP, pltpu.roll(one, CAP, 1), two)
         value_parts.append(jnp.concatenate([upper, lower], axis=0))
-    row_of = jnp.broadcast_to(jnp.concatenate(row_parts, axis=1) // 4, (C_OBS, SLOTS)).astype(F32).astype(BF16)
+    row_of = jnp.broadcast_to(jnp.concatenate(row_parts, axis=1) // 4, (C_OBS, slots)).astype(F32).astype(BF16)
     values = jnp.concatenate(value_parts, axis=1).astype(BF16)
     zero = jnp.zeros_like(values)
     for r in range(ROWS):
-        lhs_ref[r * C_OBS : (r + 1) * C_OBS, :] = jnp.where(row_of == jnp.array(r, BF16), values, zero)
-    rows = lax.broadcasted_iota(jnp.int32, (ROWS, SLOTS), 0).astype(F32).astype(BF16)
-    lhs_ref[ROWS * C_OBS :, :] = jnp.where(row_of == rows, jnp.ones_like(values), zero)
+        lhs_ref[r * C_OBS : (r + 1) * C_OBS, :slots] = jnp.where(row_of == jnp.array(r, BF16), values, zero)
+    rows = lax.broadcasted_iota(jnp.int32, (ROWS, slots), 0).astype(F32).astype(BF16)
+    lhs_ref[ROWS * C_OBS :, :slots] = jnp.where(row_of == rows, jnp.ones_like(values), zero)
     quarter = lax.rem(codes, 4).astype(F32).T
     lane_quarter = (lax.broadcasted_iota(jnp.int32, (CAP, N), 1) // 32).astype(F32)
-    for s in range(GROUP):
+    for s in range(group):
         keep = jnp.where(quarter[:CAP, s : s + 1] == lane_quarter, 1.0, 0.0).astype(BF16)
-        pixels = jnp.dot(got_w[first + s], perm_ref[...], preferred_element_type=F32).astype(BF16)
+        pixels = jnp.dot(got[first + s, :CAP, :], perm_ref[...], preferred_element_type=F32).astype(BF16)
         for phase in range(4):
             rhs_ref[s * CAP : (s + 1) * CAP, phase * N : (phase + 1) * N] = (
                 pixels[:, phase * N : (phase + 1) * N] * keep
             )
-    acc_ref[...] += jnp.dot(lhs_ref[...], rhs_ref[...], preferred_element_type=F32)
+    acc_ref[...] += jnp.dot(lhs_ref[:, :slots], rhs_ref[:slots, :], preferred_element_type=F32)
 
 
 def send_to(source, target, sent, came, device):
@@ -103,40 +94,43 @@
     )
 
 
-def all_sum(lat, lon, part_ref, total_ref, by_lat, by_y, by_x, sent, came):
-    x, y = lon // 4, lax.rem(lon, 4)
-    rows = lambda at: pl.ds(pl.multiple_of(8 * at, 8), 8)
+def all_sum(lat, lon, part_ref, total_ref, by_lon, by_lat, sent, came):
+    def piece(ref, p):
+        rows = pl.ds(pl.multiple_of(8 * (p // 2), 8), 8)
+        return ref.at[rows, pl.ds(pl.multiple_of(512 * lax.rem(p, 2), 512), 512)]
+
+    copies = []
+    for d in range(1, 16):
+        to = lax.rem(lon + d, 16)
+        copies.append(send_to(piece(part_ref, to), by_lon.at[d], sent.at[d], came.at[d], (lat, to)))
+    for copy in copies:
+        copy.start()
+    total = piece(part_ref, lon)[...]
+    for d in range(1, 16):
+        copies[d - 1].wait()
+        total = total + by_lon[d]
+    by_lat[lat] = total
     copies = []
     for d in range(1, 8):
         to = lax.rem(lat + d, 8)
-        copies.append(send_to(part_ref.at[rows(to)], by_lat.at[d], sent.at[d], came.at[d], (to, lon)))
+        copies.append(send_to(by_lat.at[lat], by_lat.at[lat], sent.at[16 + d], came.at[16 + d], (to, lon)))
     for copy in copies:
         copy.start()
     for copy in copies:
         copy.wait()
-    total = part_ref[rows(lat), :]
+    total = by_lat[0]
     for d in range(1, 8):
         total = total + by_lat[d]
-    for base, slots, here in ((8, by_y, y), (12, by_x, x)):
-        slots[here] = total
-        copies = []
-        for d in range(1, 4):
-            to_lon = x * 4 + lax.rem(y + d, 4) if base == 8 else lax.rem(x + d, 4) * 4 + y
-            copies.append(send_to(slots.at[here], slots.at[here], sent.at[base + d], came.at[base + d], (lat, to_lon)))
-        for copy in copies:
-            copy.start()
-        for copy in copies:
-            copy.wait()
-        total = (slots[0] + slots[1]) + (slots[2] + slots[3])
-    total_ref[rows(lat), :] = total
+    mine = piece(total_ref, lon)
+    mine[...] = total
     copies = []
-    for d in range(1, 8):
-        to = lax.rem(lat + d, 8)
-        copies.append(send_to(total_ref.at[rows(lat)], total_ref.at[rows(lat)], sent.at[16 + d], came.at[16 + d], (to, lon)))
+    for d in range(1, 16):
+        copies.append(send_to(mine, mine, sent.at[24 + d], came.at[24 + d], (lat, lax.rem(lon + d, 16))))
     for copy in copies:
         copy.start()
     for copy in copies:
         copy.wait()
+
 
 CH = 64
 STEP_ONE = 5 * C_OBS
@@ -236,14 +230,6 @@
     lax.fori_loop(0, 4, pair, 0)
 
 
-def split_row(r, rows_of, edge, high_ref, low_ref):
-    phases = [rows_of(phase) for phase in range(4)]
-    taps = [enter_west(phases[3], edge)] + phases
-    high, low = halves(jnp.concatenate(taps, axis=0))
-    high_ref[r] = high
-    low_ref[r] = low
-
-
 def field_edges(acc_ref, edge_ref):
     packed = jnp.zeros((C_OBS, N), F32)
     for r in range(ROWS):
@@ -252,23 +238,32 @@
     edge_ref[C_OBS:, :] = acc_ref[ROWS * C_OBS :, 3 * N :]
 
 
-def split_field(lat, acc_ref, north, north_thin, from_west, from_corner, thin, high_ref, low_ref, thin_high, thin_low):
+def split_inside(acc_ref, thin, high_ref, low_ref):
     for r in range(ROWS):
-        split_row(
-            r + 1,
-            lambda phase, r=r: acc_ref[r * C_OBS : (r + 1) * C_OBS, phase * N : (phase + 1) * N],
-            from_west[:C_OBS, r : r + 1], high_ref, low_ref,
-        )
-    inside = lat > 0
-    split_row(
-        0,
-        lambda phase: jnp.where(inside, north[:, phase * N : (phase + 1) * N], 0.0),
-        jnp.where(inside, from_corner[:C_OBS, ROWS - 1 : ROWS], 0.0), high_ref, low_ref,
-    )
+        for phase in range(4):
+            high, low = halves(acc_ref[r * C_OBS : (r + 1) * C_OBS, phase * N : (phase + 1) * N])
+            at = slice((phase + 1) * C_OBS, (phase + 2) * C_OBS)
+            high_ref[r + 1, at, :] = high
+            low_ref[r + 1, at, :] = low
     thin[...] = jnp.zeros_like(thin)
     for phase in range(4):
+        thin[1 : ROWS + 1, phase + 1, :] = acc_ref[ROWS * C_OBS :, phase * N : (phase + 1) * N]
+
+
+def split_rim(lat, acc_ref, north, north_thin, from_west, from_corner, thin, high_ref, low_ref, thin_high, thin_low):
+    for r in range(ROWS):
+        moved = enter_west(acc_ref[r * C_OBS : (r + 1) * C_OBS, 3 * N :], from_west[:C_OBS, r : r + 1])
+        high, low = halves(moved)
+        high_ref[r + 1, :C_OBS, :] = high
+        low_ref[r + 1, :C_OBS, :] = low
+    inside = lat > 0
+    phases = [jnp.where(inside, north[:, phase * N : (phase + 1) * N], 0.0) for phase in range(4)]
+    corner = jnp.where(inside, from_corner[:C_OBS, ROWS - 1 : ROWS], 0.0)
+    high, low = halves(jnp.concatenate([enter_west(phases[3], corner)] + phases, axis=0))
+    high_ref[0] = high
+    low_ref[0] = low
+    for phase in range(4):
         at = slice(phase * N, (phase + 1) * N)
-        thin[1 : ROWS + 1, phase + 1, :] = acc_ref[ROWS * C_OBS :, at]
         thin[0, phase + 1 : phase + 2, :] = jnp.where(inside, north_thin[7:8, at], 0.0)
     thin[1 : ROWS + 1, 0, :] = enter_west(acc_ref[ROWS * C_OBS :, 3 * N :], from_west[C_OBS:, N - 1 :])
     corner = enter_west(north_thin[7:8, 3 * N :], from_corner[2 * C_OBS - 1 :, N - 1 :])
@@ -366,7 +361,7 @@
         ),
     )
     shifted = pltpu.roll(tight, CH, 1)
-    part_ref[:, 4 * N : 7 * N] = shifted[:, : 3 * N]
+    part_ref[:, 4 * N :] = shifted
     part_ref[:, : 9 * CH] = two
 
 
@@ -380,10 +375,10 @@
         one_ref[i, C_OBS:, :] = turned[thin : thin + 1]
 
 
-def phase_picker():
-    lane = jnp.arange(4 * N, dtype=jnp.int32)
-    source = 4 * (lane % 32) + lane // N
-    return (jnp.arange(N, dtype=jnp.int32)[:, None] == source[None, :]).astype(BF16)
+def arrange_picker(picker_ref):
+    lane = lax.broadcasted_iota(jnp.int32, (N, 4 * N), 1)
+    pixel = lax.broadcasted_iota(jnp.int32, (N, 4 * N), 0)
+    picker_ref[...] = jnp.where(pixel == 4 * lax.rem(lane, 32) + lane // N, 1.0, 0.0).astype(BF16)
 
 
 class Named:
@@ -394,11 +389,10 @@
 SCRATCH = {
     "wide": pltpu.VMEM((CAP, C_OBS, N), F32),
     "turned": pltpu.VMEM((N, 16, N), F32),
-    "packed": pltpu.VMEM((N, 16, N), BF16),
     "codes": pltpu.VMEM((N, 1, N), jnp.int32),
-    "got_w": pltpu.VMEM((N, CAP, N), BF16),
-    "got_v": pltpu.VMEM((N, 16, N), BF16),
-    "got_c": pltpu.VMEM((N, 1, N), jnp.int32),
+    "got_codes": pltpu.VMEM((N, 1, N), jnp.int32),
+    "message": pltpu.VMEM((N, SENT, N), BF16),
+    "got": pltpu.VMEM((N, SENT, N), BF16),
     "lhs": pltpu.VMEM((ROWS * C_OBS + ROWS, SLOTS), BF16),
     "rhs": pltpu.VMEM((SLOTS, 4 * N), BF16),
     "acc": pltpu.VMEM((ROWS * C_OBS + ROWS, 4 * N), F32),
@@ -434,71 +428,103 @@
     "act_north": pltpu.VMEM((N, N), F32),
     "act_high": pltpu.VMEM((ROWS // 2 + 1, STEP_TWO, N), BF16),
     "act_low": pltpu.VMEM((ROWS // 2 + 1, STEP_TWO, N), BF16),
+    "grad_one": pltpu.VMEM((9, C_OBS + 1, CH), F32),
+    "grad_two": pltpu.VMEM((9, CH, CH), F32),
+    "features": pltpu.VMEM((CH, 8, N), BF16),
     "wide_features": pltpu.VMEM((CH, 8, N), F32),
-    "part": pltpu.VMEM((CH, 7 * N), F32),
-    "total": pltpu.VMEM((CH, 7 * N), F32),
-    "by_lat": pltpu.VMEM((8, 8, 7 * N), F32),
-    "by_y": pltpu.VMEM((4, 8, 7 * N), F32),
-    "by_x": pltpu.VMEM((4, 8, 7 * N), F32),
-    "sent": pltpu.SemaphoreType.DMA((3,)),
-    "came_w": pltpu.SemaphoreType.DMA((STEPS,)),
-    "came_v": pltpu.SemaphoreType.DMA((STEPS,)),
-    "came_c": pltpu.SemaphoreType.DMA((STEPS,)),
-    "own": pltpu.SemaphoreType.DMA((3,)),
+    "part": pltpu.VMEM((CH, 8 * N), F32),
+    "total": pltpu.VMEM((CH, 8 * N), F32),
+    "by_lon": pltpu.VMEM((16, 8, 4 * N), F32),
+    "by_lat": pltpu.VMEM((8, 8, 4 * N), F32),
+    "sent": pltpu.SemaphoreType.DMA((2,)),
+    "came": pltpu.SemaphoreType.DMA((2, STEPS + 2)),
+    "values": pltpu.VMEM((CAP, C_OBS, N), BF16),
+    "blocks": pltpu.VMEM((CAP, N), jnp.int32),
+    "counts": pltpu.VMEM((1, N), jnp.int32),
+    "cot_in": pltpu.VMEM((CH, 8, N), BF16),
+    "one": pltpu.VMEM((3, 3, C_OBS + 1, CH), F32),
+    "two": pltpu.VMEM((3, 3, CH, CH), F32),
+    "picker": pltpu.VMEM((N, 4 * N), BF16),
+    "fetch": pltpu.SemaphoreType.DMA((7,)),
+    "met": pltpu.SemaphoreType.REGULAR,
+    "own": pltpu.SemaphoreType.DMA((2,)),
+    "result": pltpu.SemaphoreType.DMA((3,)),
     "halo_sent": pltpu.SemaphoreType.DMA((10,)),
     "halo_came": pltpu.SemaphoreType.DMA((10,)),
-    "sum_sent": pltpu.SemaphoreType.DMA((24,)),
-    "sum_came": pltpu.SemaphoreType.DMA((24,)),
+    "sum_sent": pltpu.SemaphoreType.DMA((40,)),
+    "sum_came": pltpu.SemaphoreType.DMA((40,)),
 }
 
 
 def whole_kernel(
-    values_ref, w_ref, blocks_ref, counts_ref, perm_ref, one_ref, two_ref, cot_ref,
+    values_ref, w_ref, blocks_ref, counts_ref, one_ref, two_ref, cot_ref,
     features_ref, grad_one_ref, grad_two_ref, *scratch,
 ):
     m = Named(SCRATCH, scratch)
     lat, lon = position()
     me = lat * 16 + lon
-    barrier = greet_all(lat, lon)
-    pack_values(values_ref, m.wide, m.turned, m.packed)
-    pack_codes(blocks_ref, counts_ref, m.codes)
-    arrange_cotangent(cot_ref, m.wide_cot, m.cot, m.cot_col)
-    arrange_kernels(one_ref, two_ref, m.wide_one, m.wide_adj, m.wide_two, m.left_one, m.left_adj, m.left_two)
-    m.acc[...] = jnp.zeros_like(m.acc)
+    barrier = greet_near(lat, lon)
+    fetched = [
+        pltpu.make_async_copy(source, target, m.fetch.at[k])
+        for k, (source, target) in enumerate((
+            (values_ref, m.values), (blocks_ref, m.blocks), (counts_ref, m.counts),
+            (w_ref, m.message.at[:, pl.ds(0, CAP)]),
+            (cot_ref, m.cot_in), (one_ref, m.one), (two_ref, m.two),
+        ))
+    ]
+    for copy in fetched:
+        copy.start()
+    arrange_picker(m.picker)
+
+    north, south = lax.rem(lat + 7, 8), lax.rem(lat + 1, 8)
+    west, east = lax.rem(lon + 15, 16), lax.rem(lon + 1, 16)
+
+    def halo(k, source, target, device):
+        return send_to(source, target, m.halo_sent.at[k], m.halo_came.at[k], device)
+
+    pl.semaphore_wait(barrier, NEAR)
+    for d in range(1, 16):
+        pl.semaphore_signal(m.met, inc=1, device_id=(lat, lax.rem(lon + d, 16)), device_id_type=MESH)
+    fetched[0].wait()
+    m.wide[...] = m.values[...].astype(F32)
+    pack_values(m.wide, m.turned, m.message)
+    fetched[1].wait()
+    fetched[2].wait()
+    pack_codes(m.blocks, m.counts, m.codes)
+    fetched[3].wait()
+    streams = ((m.message, m.got), (m.codes, m.got_codes))
     mine = [
-        pltpu.make_async_copy(w_ref.at[me], m.got_w.at[0], m.own.at[0]),
-        pltpu.make_async_copy(m.packed.at[me], m.got_v.at[0], m.own.at[1]),
-        pltpu.make_async_copy(m.codes.at[me], m.got_c.at[0], m.own.at[2]),
+        pltpu.make_async_copy(source.at[me], target.at[0], m.own.at[k]) for k, (source, target) in enumerate(streams)
     ]
     for copy in mine:
         copy.start()
-
-    north, south = lax.rem(lat + 7, 8), lax.rem(lat + 1, 8)
-    west, east = lax.rem(lon + 15, 16), lax.rem(lon + 1, 16)
-
-    def halo(k, source, target, device):
-        return send_to(source, target, m.halo_sent.at[k], m.halo_came.at[k], device)
-
+    def send(ordinal, carry):
+        to_lat, to_lon = partner(lat, lon, ordinal)
+        step = jnp.where(ordinal < STEPS * GROUP, ordinal // GROUP, ordinal // (GROUP // 2) - STEPS)
+        to = to_lat * 16 + to_lon
+        for k, (source, target) in enumerate(streams):
+            send_to(
+                source.at[to], target.at[ordinal], m.sent.at[k], m.came.at[k, step], (to_lat, to_lon)
+            ).start()
+        return carry
+
+    fetched[4].wait()
+    arrange_cotangent(m.cot_in, m.wide_cot, m.cot, m.cot_col)
     cot_halo = [
         halo(0, m.cot_col, m.cot_east, (lat, west)),
         halo(1, m.cot.at[0], m.cot_south, (north, lon)),
         halo(2, m.cot_col, m.cot_corner, (north, west)),
     ]
-    pl.semaphore_wait(barrier, N - 1)
-    for copy in cot_halo:
-        copy.start()
-
-    streams = ((w_ref, m.got_w, m.came_w), (m.packed, m.got_v, m.came_v), (m.codes, m.got_c, m.came_c))
-
-    def send(ordinal, carry):
-        to_lat, to_lon = partner(lat, lon, ordinal, 1)
-        to = to_lat * 16 + to_lon
-        step = ordinal // GROUP
-        for k, (source, target, came) in enumerate(streams):
-            send_to(source.at[to], target.at[ordinal], m.sent.at[k], came.at[step], (to_lat, to_lon)).start()
-        return carry
-
+    cot_halo[0].start()
+    cot_halo[1].start()
+    pl.semaphore_wait(m.met, 15)
+    cot_halo[2].start()
     lax.fori_loop(1, N, send, 0)
+
+    fetched[5].wait()
+    fetched[6].wait()
+    arrange_kernels(m.one, m.two, m.wide_one, m.wide_adj, m.wide_two, m.left_one, m.left_adj, m.left_two)
+    m.acc[...] = jnp.zeros_like(m.acc)
     for copy in cot_halo:
         copy.wait()
     back_to_activation(
@@ -508,10 +534,12 @@
         copy.wait()
 
     def arrive(first, count, step):
-        for source, target, came in streams:
-            pltpu.make_async_copy(
-                target.at[pl.ds(first, count)], target.at[pl.ds(first, count)], came.at[step]
-            ).wait()
+        for k, (_, target) in enumerate(streams):
+            part = target.at[pl.ds(first, count)]
+            pltpu.make_async_copy(part, part, m.came.at[k, step]).wait()
+
+    def spread(first, group):
+        spread_group(first, group, m.got, m.got_codes, m.picker, m.lhs, m.rhs, m.acc)
 
     def work(step, carry):
         @pl.when(step == 0)
@@ -522,10 +550,18 @@
         def _():
             arrive(step * GROUP, GROUP, step)
 
-        spread_group(step, m.got_w, m.got_v, m.got_c, perm_ref, m.lhs, m.rhs, m.acc)
+        spread(step * GROUP, GROUP)
         return carry
 
     lax.fori_loop(0, STEPS, work, 0)
+
+    def work_half(step, carry):
+        first = STEPS * GROUP + step * (GROUP // 2)
+        arrive(first, GROUP // 2, STEPS + step)
+        spread(first, GROUP // 2)
+        return carry
+
+    lax.fori_loop(0, 2, work_half, 0)
 
     last = ROWS * C_OBS
     rows_halo = [
@@ -541,9 +577,10 @@
     field_edges(m.acc, m.edge)
     for copy in edge_halo:
         copy.start()
+    split_inside(m.acc, m.thin, m.field_high, m.field_low)
     for copy in edge_halo + rows_halo:
         copy.wait()
-    split_field(
+    split_rim(
         lat, m.acc, m.north, m.north_thin, m.edge_west, m.edge_corner, m.thin,
         m.field_high, m.field_low, m.thin_high, m.thin_low,
     )
@@ -564,26 +601,43 @@
     split_activation(lat, m.act, m.act_north, m.act_west, m.act_corner, m.act_high, m.act_low)
     grad_two = second_layer(m.act_high, m.act_low, m.left_two, m.cot, m.wide_features)
     pack_gradients(grad_one, grad_two, m.part)
-    features_ref[...] = m.wide_features[...].astype(BF16)
-    all_sum(lat, lon, m.part, m.total, m.by_lat, m.by_y, m.by_x, m.sum_sent, m.sum_came)
-    unpack_gradients(m.total, grad_one_ref, grad_two_ref)
-    for k, (_, target, _) in enumerate(streams):
-        pltpu.make_async_copy(target.at[pl.ds(0, N - 1)], target.at[pl.ds(0, N - 1)], m.sent.at[k]).wait()
+    m.features[...] = m.wide_features[...].astype(BF16)
+    results = [
+        pltpu.make_async_copy(m.features, features_ref, m.result.at[0]),
+        pltpu.make_async_copy(m.grad_one, grad_one_ref, m.result.at[1]),
+        pltpu.make_async_copy(m.grad_two, grad_two_ref, m.result.at[2]),
+    ]
+    results[0].start()
+    all_sum(lat, lon, m.part, m.total, m.by_lon, m.by_lat, m.sum_sent, m.sum_came)
+    unpack_gradients(m.total, m.grad_one, m.grad_two)
+    results[1].start()
+    results[2].start()
+    for k, (_, target) in enumerate(streams):
+        everything = target.at[pl.ds(0, N - 1)]
+        pltpu.make_async_copy(everything, everything, m.sent.at[k]).wait()
+    for copy in results:
+        copy.wait()
+
+
+def hand_on_kernel(*refs):
+    for k in range(3):
+        refs[3 + k][...] = refs[k][...]
 
 
 def on_device(
     obs_values, kernel_weights, pixel_blocks, obs_counts, kernel_one, kernel_two, cotangent
 ):
-    vmem = pl.BlockSpec(memory_space=pltpu.VMEM)
-    features, grad_one, grad_two = pl.pallas_call(
+    vmem, anywhere = pl.BlockSpec(memory_space=pltpu.VMEM), pl.BlockSpec(memory_space=pl.ANY)
+    outputs = (
+        jax.ShapeDtypeStruct((CH, 8, N), BF16),
+        jax.ShapeDtypeStruct((9, C_OBS + 1, CH), F32),
+        jax.ShapeDtypeStruct((9, CH, CH), F32),
+    )
+    results = pl.pallas_call(
         whole_kernel,
-        out_shape=(
-            jax.ShapeDtypeStruct((CH, 8, N), BF16),
-            jax.ShapeDtypeStruct((9, C_OBS + 1, CH), F32),
-            jax.ShapeDtypeStruct((9, CH, CH), F32),
-        ),
-        in_specs=[vmem, pl.BlockSpec(memory_space=pl.ANY)] + [vmem] * 6,
-        out_specs=(vmem, vmem, vmem),
+        out_shape=outputs,
+        in_specs=[anywhere] * 7,
+        out_specs=(anywhere,) * 3,
         scratch_shapes=list(SCRATCH.values()),
         compiler_params=pltpu.CompilerParams(collective_id=0, has_side_effects=True, vmem_limit_bytes=56 << 20),
     )(
@@ -591,11 +645,17 @@
         kernel_weights[0],
         pixel_blocks[0].T,
         obs_counts,
-        phase_picker(),
         kernel_one.transpose(0, 1, 3, 2),
         kernel_two,
         cotangent,
     )
+    features, grad_one, grad_two = pl.pallas_call(
+        hand_on_kernel,
+        out_shape=outputs,
+        in_specs=[vmem] * 3,
+        out_specs=(vmem,) * 3,
+        scratch_shapes=[pltpu.SemaphoreType.DMA((3,))],
+    )(*results)
     grad_one = grad_one.reshape(3, 3, C_OBS + 1, CH).transpose(0, 1, 3, 2)
     return features, grad_one, grad_two.reshape(3, 3, CH, CH)
 

time: 86.3 us -> 81.5 us (0.944)
  local copies, waits for them, and re-layouts: 4.87 us -> 0 us
  Pallas kernels: 79.9 us -> 80.8 us
    unnamed x3 -> x0, local copies, waits for them, and re-layouts: 4.87 us -> none
    pallas_call x1 -> x2, Pallas kernels: 79.9 us -> 80.8 us  [the longest x1 78.8 us: on_device(): pl.pallas_call(whole_kernel, out_shape=outputs, in_specs=[anywhere] * 7,...]
where the time goes in v1:
time: 81.5 us; the launch traced here: 81.4 us
  Pallas kernels  80.8 us (99%)
    pallas_call x1, Pallas kernels, on_device(): pl.pallas_call(whole_kernel, out_shape=outputs, in_specs=[anywhere] * 7,...  78.8 us
    pallas_call x1, Pallas kernels, on_device(): pl.pallas_call(hand_on_kernel, out_shape=outputs, in_specs=[vmem] * 3, ou...  1.98 us

profile of v1, /device:TPU:1, one launch (start us, length us, event | category | flops | bytes accessed | tf_op | source)
XLA Modules:
  0.0 81.4 jit_solution(11728705884013785173)
XLA Ops:
  0.6 78.8 %shard_map.94 = (bf16[64,8,128]{2,1,0:T(8,128)(2,1)}, f32[9,33,64]{2,1,0:T(8,128)}, f32[9,64,64]{2,1,0:T(8,128)}) custom-call(bf16[64,32,128]{2,1,0:T(8,128)(2,1)} %bitcast.13, bf16[128,64,128]{2,1,0:T(8,128)(2,1)} %bitcast.12, s32[64,128]{1,0:T(8,128)} %bitcast.15, s32[1,128]{1,0:T(1,128)} %counts_ref.1, f32[3,3,33,64]{3,2,1,0:T(8,128)} %bitcast.14, ...), custom_call_target="tpu_custom_call" | custom-call | tf_op jit(solution)/shard_map/pallas_call | solution.py:636
  79.4 2.0 %shard_map.95 = (bf16[64,8,128]{2,1,0:T(8,128)(2,1)}, f32[9,33,64]{2,1,0:T(8,128)}, f32[9,64,64]{2,1,0:T(8,128)}) custom-call(bf16[64,8,128]{2,1,0:T(8,128)(2,1)} %get-tuple-element.9.refs_0_, f32[9,33,64]{2,1,0:T(8,128)} %get-tuple-element.10.refs_1_, f32[9,64,64]{2,1,0:T(8,128)} %get-tuple-element.11.refs_2_), custom_call_target="tpu_custom_call" | custom-call | tf_op jit(solution)/shard_map/pallas_call | solution.py:652

commit v2 on v1

--- a/solution.py
+++ b/solution.py
@@ -94,42 +94,50 @@
     )
 
 
-def all_sum(lat, lon, part_ref, total_ref, by_lon, by_lat, sent, came):
-    def piece(ref, p):
-        rows = pl.ds(pl.multiple_of(8 * (p // 2), 8), 8)
-        return ref.at[rows, pl.ds(pl.multiple_of(512 * lax.rem(p, 2), 512), 512)]
-
+def sixteenth(ref, p):
+    rows = pl.ds(pl.multiple_of(8 * (p // 2), 8), 8)
+    return ref.at[rows, pl.ds(pl.multiple_of(512 * lax.rem(p, 2), 512), 512)]
+
+
+def sum_begin(lat, lon, part_ref, by_lon, sent, came):
     copies = []
     for d in range(1, 16):
         to = lax.rem(lon + d, 16)
-        copies.append(send_to(piece(part_ref, to), by_lon.at[d], sent.at[d], came.at[d], (lat, to)))
+        copies.append(send_to(sixteenth(part_ref, to), by_lon.at[d], sent.at[d], came.at[d], (lat, to)))
     for copy in copies:
         copy.start()
-    total = piece(part_ref, lon)[...]
+    return copies
+
+
+def sum_end(lat, lon, copies, part_ref, total_ref, by_lon, by_lat, sent, came):
+    for copy in copies:
+        copy.wait_recv()
+    total = sixteenth(part_ref, lon)[...]
     for d in range(1, 16):
-        copies[d - 1].wait()
         total = total + by_lon[d]
     by_lat[lat] = total
-    copies = []
+    across = []
     for d in range(1, 8):
         to = lax.rem(lat + d, 8)
-        copies.append(send_to(by_lat.at[lat], by_lat.at[lat], sent.at[16 + d], came.at[16 + d], (to, lon)))
-    for copy in copies:
+        across.append(send_to(by_lat.at[lat], by_lat.at[lat], sent.at[16 + d], came.at[16 + d], (to, lon)))
+    for copy in across:
         copy.start()
-    for copy in copies:
-        copy.wait()
+    for copy in across:
+        copy.wait_recv()
     total = by_lat[0]
     for d in range(1, 8):
         total = total + by_lat[d]
-    mine = piece(total_ref, lon)
+    mine = sixteenth(total_ref, lon)
     mine[...] = total
-    copies = []
+    back = []
     for d in range(1, 16):
-        copies.append(send_to(mine, mine, sent.at[24 + d], came.at[24 + d], (lat, lax.rem(lon + d, 16))))
-    for copy in copies:
+        back.append(send_to(mine, mine, sent.at[24 + d], came.at[24 + d], (lat, lax.rem(lon + d, 16))))
+    for copy in back:
         copy.start()
-    for copy in copies:
-        copy.wait()
+    for copy in back:
+        copy.wait_recv()
+    for copy in copies + across + back:
+        copy.wait_send()
 
 
 CH = 64
@@ -297,7 +305,7 @@
             act[2 * p + k] = active[:, k * N : (k + 1) * N]
         return carry
 
-    lax.fori_loop(0, ROWS // 4, pair, 0)
+    lax.fori_loop(0, ROWS // 4, pair, 0, unroll=4)
 
 
 def first_gradient(field_high, field_low, thin_high, thin_low, pre, grad_act):
@@ -313,7 +321,7 @@
         both = dot_nt(jnp.concatenate([high, low], axis=0), field)
         return total + (both[:N] + both[N:]) + dot_nt(high, beside(taps_one, p, field_low, thin_low))
 
-    return lax.fori_loop(0, ROWS // 4, pair, jnp.zeros((N, 4 * N), F32))
+    return lax.fori_loop(0, ROWS // 4, pair, jnp.zeros((N, 4 * N), F32), unroll=4)
 
 
 def activation_edges(act, edge_ref):
@@ -323,32 +331,43 @@
     edge_ref[...] = packed
 
 
-def split_activation(lat, act, north, from_west, from_corner, high_ref, low_ref):
-    def one(place, value, column):
-        high, low = halves(jnp.concatenate([enter_west(value[CH:], column), value], axis=0))
-        high_ref[place] = high
-        low_ref[place] = low
-
+def split_activation_inside(act, high_ref, low_ref):
     for y in range(ROWS // 2):
-        one(y + 1, act[y], from_west[:, y : y + 1])
+        high, low = halves(act[y])
+        high_ref[y + 1, CH:, :] = high
+        low_ref[y + 1, CH:, :] = low
+
+
+def split_activation_rim(lat, act, north, from_west, from_corner, high_ref, low_ref):
+    for y in range(ROWS // 2):
+        high, low = halves(enter_west(act[y, CH:, :], from_west[:, y : y + 1]))
+        high_ref[y + 1, :CH, :] = high
+        low_ref[y + 1, :CH, :] = low
     last = ROWS // 2 - 1
-    one(0, jnp.where(lat > 0, north[...], 0.0), jnp.where(lat > 0, from_corner[:, last : last + 1], 0.0))
-
-
-def second_layer(act_high, act_low, left_two, cot, wide_features):
+    value = jnp.where(lat > 0, north[...], 0.0)
+    column = jnp.where(lat > 0, from_corner[:, last : last + 1], 0.0)
+    high, low = halves(jnp.concatenate([enter_west(value[CH:], column), value], axis=0))
+    high_ref[0] = high
+    low_ref[0] = low
+
+
+def second_gradient(act_high, act_low, cot):
     total = jnp.zeros((CH, 9 * CH), F32)
     for p in range(4):
-        high, low = beside(taps_two, p, act_high), beside(taps_two, p, act_low)
-        both = dot(left_two[...], high)
-        out = both[:CH] + both[CH:] + dot(left_two[:CH, :], low)
+        grad = jnp.concatenate([cot[2 * p], cot[2 * p + 1]], axis=1).astype(BF16)
+        total = total + (dot_nt(grad, beside(taps_two, p, act_high)) + dot_nt(grad, beside(taps_two, p, act_low)))
+    return total
+
+
+def second_layer(act_high, act_low, left_two, wide_features):
+    for p in range(4):
+        both = dot(left_two[...], beside(taps_two, p, act_high))
+        out = both[:CH] + both[CH:] + dot(left_two[:CH, :], beside(taps_two, p, act_low))
         for k in range(2):
             wide_features[:, 2 * p + k, :] = out[:, k * N : (k + 1) * N]
-        grad = jnp.concatenate([cot[2 * p], cot[2 * p + 1]], axis=1).astype(BF16)
-        total = total + (dot_nt(grad, high) + dot_nt(grad, low))
-    return total
-
-
-def pack_gradients(one, two, part_ref):
+
+
+def pack_first_gradient(one, part_ref):
     lane = lax.broadcasted_iota(jnp.int32, (CH, 4 * N), 1)
     upper, lower = one[:CH], one[CH:]
     moved = jnp.where(lane < 3 * STEP_ONE, pltpu.roll(lower, 4 * N - 2 * C_OBS, 1), pltpu.roll(lower, 4 * N - 2, 1))
@@ -362,7 +381,6 @@
     )
     shifted = pltpu.roll(tight, CH, 1)
     part_ref[:, 4 * N :] = shifted
-    part_ref[:, : 9 * CH] = two
 
 
 def unpack_gradients(total_ref, one_ref, two_ref):
@@ -596,11 +614,14 @@
     act_halo[1].start()
     act_halo[2].start()
     grad_one = first_gradient(*field, m.pre, m.grad_act)
+    pack_first_gradient(grad_one, m.part)
+    split_activation_inside(m.act, m.act_high, m.act_low)
     for copy in act_halo:
         copy.wait()
-    split_activation(lat, m.act, m.act_north, m.act_west, m.act_corner, m.act_high, m.act_low)
-    grad_two = second_layer(m.act_high, m.act_low, m.left_two, m.cot, m.wide_features)
-    pack_gradients(grad_one, grad_two, m.part)
+    split_activation_rim(lat, m.act, m.act_north, m.act_west, m.act_corner, m.act_high, m.act_low)
+    m.part[:, : 9 * CH] = second_gradient(m.act_high, m.act_low, m.cot)
+    first_leg = sum_begin(lat, lon, m.part, m.by_lon, m.sum_sent, m.sum_came)
+    second_layer(m.act_high, m.act_low, m.left_two, m.wide_features)
     m.features[...] = m.wide_features[...].astype(BF16)
     results = [
         pltpu.make_async_copy(m.features, features_ref, m.result.at[0]),
@@ -608,7 +629,7 @@
         pltpu.make_async_copy(m.grad_two, grad_two_ref, m.result.at[2]),
     ]
     results[0].start()
-    all_sum(lat, lon, m.part, m.total, m.by_lon, m.by_lat, m.sum_sent, m.sum_came)
+    sum_end(lat, lon, first_leg, m.part, m.total, m.by_lon, m.by_lat, m.sum_sent, m.sum_came)
     unpack_gradients(m.total, m.grad_one, m.grad_two)
     results[1].start()
     results[2].start()

time: 81.5 us -> 80 us (0.982)
  Pallas kernels: 80.8 us -> 79.3 us
    pallas_call x1, Pallas kernels: 78.8 us -> 77.3 us  [on_device(): pl.pallas_call(whole_kernel, out_shape=outputs, in_specs=[anywhere] * 7,...]
where the time goes in v2:
time: 80 us; the launch traced here: 79.9 us
  Pallas kernels  79.3 us (99%)
    pallas_call x1, Pallas kernels, on_device(): pl.pallas_call(whole_kernel, out_shape=outputs, in_specs=[anywhere] * 7,...  77.3 us
    pallas_call x1, Pallas kernels, on_device(): pl.pallas_call(hand_on_kernel, out_shape=outputs, in_specs=[vmem] * 3, ou...  1.98 us

profile of v2, /device:TPU:1, one launch (start us, length us, event | category | flops | bytes accessed | tf_op | source)
XLA Modules:
  0.0 79.9 jit_solution(12372617827888562201)
XLA Ops:
  0.6 77.3 %shard_map.94 = (bf16[64,8,128]{2,1,0:T(8,128)(2,1)}, f32[9,33,64]{2,1,0:T(8,128)}, f32[9,64,64]{2,1,0:T(8,128)}) custom-call(bf16[64,32,128]{2,1,0:T(8,128)(2,1)} %bitcast.13, bf16[128,64,128]{2,1,0:T(8,128)(2,1)} %bitcast.12, s32[64,128]{1,0:T(8,128)} %bitcast.15, s32[1,128]{1,0:T(1,128)} %counts_ref.1, f32[3,3,33,64]{3,2,1,0:T(8,128)} %bitcast.14, ...), custom_call_target="tpu_custom_call" | custom-call | tf_op jit(solution)/shard_map/pallas_call | solution.py:657
  77.9 2.0 %shard_map.95 = (bf16[64,8,128]{2,1,0:T(8,128)(2,1)}, f32[9,33,64]{2,1,0:T(8,128)}, f32[9,64,64]{2,1,0:T(8,128)}) custom-call(bf16[64,8,128]{2,1,0:T(8,128)(2,1)} %get-tuple-element.9.refs_0_, f32[9,33,64]{2,1,0:T(8,128)} %get-tuple-element.10.refs_1_, f32[9,64,64]{2,1,0:T(8,128)} %get-tuple-element.11.refs_2_), custom_call_target="tpu_custom_call" | custom-call | tf_op jit(solution)/shard_map/pallas_call | solution.py:673

commit v3 on v2

--- a/solution.py
+++ b/solution.py
@@ -94,6 +94,16 @@
     )
 
 
+AROUND = sorted(
+    ((dx, dy) for dx in range(4) for dy in range(4) if dx + dy > 0),
+    key=lambda at: -min(at[0], 4 - at[0]) - min(at[1], 4 - at[1]),
+)
+
+
+def around(lon, at):
+    return lax.rem(lon // 4 + at[0], 4) * 4 + lax.rem(lon + at[1], 4)
+
+
 def sixteenth(ref, p):
     rows = pl.ds(pl.multiple_of(8 * (p // 2), 8), 8)
     return ref.at[rows, pl.ds(pl.multiple_of(512 * lax.rem(p, 2), 512), 512)]
@@ -101,8 +111,8 @@
 
 def sum_begin(lat, lon, part_ref, by_lon, sent, came):
     copies = []
-    for d in range(1, 16):
-        to = lax.rem(lon + d, 16)
+    for d, at in enumerate(AROUND, 1):
+        to = around(lon, at)
         copies.append(send_to(sixteenth(part_ref, to), by_lon.at[d], sent.at[d], came.at[d], (lat, to)))
     for copy in copies:
         copy.start()
@@ -130,8 +140,8 @@
     mine = sixteenth(total_ref, lon)
     mine[...] = total
     back = []
-    for d in range(1, 16):
-        back.append(send_to(mine, mine, sent.at[24 + d], came.at[24 + d], (lat, lax.rem(lon + d, 16))))
+    for d, at in enumerate(AROUND, 1):
+        back.append(send_to(mine, mine, sent.at[24 + d], came.at[24 + d], (lat, around(lon, at))))
     for copy in back:
         copy.start()
     for copy in back:

time: 80 us -> 78 us (0.975)
  Pallas kernels: 79.3 us -> 76.9 us
    pallas_call x1, Pallas kernels: 77.3 us -> 74.9 us  [on_device(): pl.pallas_call(whole_kernel, out_shape=outputs, in_specs=[anywhere] * 7,...]
where the time goes in v3:
time: 78 us; the launch traced here: 77.5 us
  Pallas kernels  76.9 us (99%)
    pallas_call x1, Pallas kernels, on_device(): pl.pallas_call(whole_kernel, out_shape=outputs, in_specs=[anywhere] * 7,...  74.9 us
    pallas_call x1, Pallas kernels, on_device(): pl.pallas_call(hand_on_kernel, out_shape=outputs, in_specs=[vmem] * 3, ou...  1.98 us

profile of v3, /device:TPU:1, one launch (start us, length us, event | category | flops | bytes accessed | tf_op | source)
XLA Modules:
  0.0 77.5 jit_solution(784776045584158070)
XLA Ops:
  0.6 74.9 %shard_map.94 = (bf16[64,8,128]{2,1,0:T(8,128)(2,1)}, f32[9,33,64]{2,1,0:T(8,128)}, f32[9,64,64]{2,1,0:T(8,128)}) custom-call(bf16[64,32,128]{2,1,0:T(8,128)(2,1)} %bitcast.13, bf16[128,64,128]{2,1,0:T(8,128)(2,1)} %bitcast.12, s32[64,128]{1,0:T(8,128)} %bitcast.15, s32[1,128]{1,0:T(1,128)} %counts_ref.1, f32[3,3,33,64]{3,2,1,0:T(8,128)} %bitcast.14, ...), custom_call_target="tpu_custom_call" | custom-call | tf_op jit(solution)/shard_map/pallas_call | solution.py:667
  75.5 2.0 %shard_map.95 = (bf16[64,8,128]{2,1,0:T(8,128)(2,1)}, f32[9,33,64]{2,1,0:T(8,128)}, f32[9,64,64]{2,1,0:T(8,128)}) custom-call(bf16[64,8,128]{2,1,0:T(8,128)(2,1)} %get-tuple-element.9.refs_0_, f32[9,33,64]{2,1,0:T(8,128)} %get-tuple-element.10.refs_1_, f32[9,64,64]{2,1,0:T(8,128)} %get-tuple-element.11.refs_2_), custom_call_target="tpu_custom_call" | custom-call | tf_op jit(solution)/shard_map/pallas_call | solution.py:683

commit v4 on v3

--- a/solution.py
+++ b/solution.py
@@ -127,8 +127,8 @@
         total = total + by_lon[d]
     by_lat[lat] = total
     across = []
-    for d in range(1, 8):
-        to = lax.rem(lat + d, 8)
+    for d, (dz, core) in enumerate(((2, 0), (2, 1), (1, 0), (3, 0), (1, 1), (3, 1), (0, 1)), 1):
+        to = lax.rem(lat // 2 + dz, 4) * 2 + lax.rem(lat + core, 2)
         across.append(send_to(by_lat.at[lat], by_lat.at[lat], sent.at[16 + d], came.at[16 + d], (to, lon)))
     for copy in across:
         copy.start()
@@ -315,7 +315,7 @@
             act[2 * p + k] = active[:, k * N : (k + 1) * N]
         return carry
 
-    lax.fori_loop(0, ROWS // 4, pair, 0, unroll=4)
+    lax.fori_loop(0, ROWS // 4, pair, 0, unroll=8)
 
 
 def first_gradient(field_high, field_low, thin_high, thin_low, pre, grad_act):
@@ -331,7 +331,7 @@
         both = dot_nt(jnp.concatenate([high, low], axis=0), field)
         return total + (both[:N] + both[N:]) + dot_nt(high, beside(taps_one, p, field_low, thin_low))
 
-    return lax.fori_loop(0, ROWS // 4, pair, jnp.zeros((N, 4 * N), F32), unroll=4)
+    return lax.fori_loop(0, ROWS // 4, pair, jnp.zeros((N, 4 * N), F32), unroll=8)
 
 
 def activation_edges(act, edge_ref):

time: 78 us -> 77.3 us (level)
  no operation moved by 1% of the time
where the time goes in v4:
time: 77.3 us; the launch traced here: 76.9 us
  Pallas kernels  76.3 us (99%)
    pallas_call x1, Pallas kernels, on_device(): pl.pallas_call(whole_kernel, out_shape=outputs, in_specs=[anywhere] * 7,...  74.3 us
    pallas_call x1, Pallas kernels, on_device(): pl.pallas_call(hand_on_kernel, out_shape=outputs, in_specs=[vmem] * 3, ou...  1.98 us

profile of v4, /device:TPU:1, one launch (start us, length us, event | category | flops | bytes accessed | tf_op | source)
XLA Modules:
  0.0 76.9 jit_solution(15472216084007649989)
XLA Ops:
  0.6 74.3 %shard_map.94 = (bf16[64,8,128]{2,1,0:T(8,128)(2,1)}, f32[9,33,64]{2,1,0:T(8,128)}, f32[9,64,64]{2,1,0:T(8,128)}) custom-call(bf16[64,32,128]{2,1,0:T(8,128)(2,1)} %bitcast.13, bf16[128,64,128]{2,1,0:T(8,128)(2,1)} %bitcast.12, s32[64,128]{1,0:T(8,128)} %bitcast.15, s32[1,128]{1,0:T(1,128)} %counts_ref.1, f32[3,3,33,64]{3,2,1,0:T(8,128)} %bitcast.14, ...), custom_call_target="tpu_custom_call" | custom-call | tf_op jit(solution)/shard_map/pallas_call | solution.py:667
  74.9 2.0 %shard_map.95 = (bf16[64,8,128]{2,1,0:T(8,128)(2,1)}, f32[9,33,64]{2,1,0:T(8,128)}, f32[9,64,64]{2,1,0:T(8,128)}) custom-call(bf16[64,8,128]{2,1,0:T(8,128)(2,1)} %get-tuple-element.9.refs_0_, f32[9,33,64]{2,1,0:T(8,128)} %get-tuple-element.10.refs_1_, f32[9,64,64]{2,1,0:T(8,128)} %get-tuple-element.11.refs_2_), custom_call_target="tpu_custom_call" | custom-call | tf_op jit(solution)/shard_map/pallas_call | solution.py:683
